TPU v7x, 32 devices: a whole 2x2x4 slice. The times are simulated.
32 devices in a mesh: ens: 2 (over x), region: 16 (over z, y, core).
Axes of the slice: x: 2, y: 2, z: 4, core: 2. Of those that a mesh axis runs over, the one named last changes fastest.
Arguments:
- node_latent: bfloat16 [16384, 512], P(('ens', 'region')), parts along dimension 0, may hold values from -6 to 6
- grid_latent: bfloat16 [16384, 512], P(('ens', 'region')), parts along dimension 0, may hold values from -6 to 6
- fine_edge_sender: int32 [65536], P(('ens', 'region')), parts along dimension 0, may hold values from 0 to 8191, as said below
- short_recv: int32 [65536], P(('ens', 'region')), parts along dimension 0, may hold values from 0 to 511
- short_geo: float32 [4, 65536], P(None, ('ens', 'region')), parts along dimension 1, may hold values from -6 to 6
- long_send: int32 [16384], P(('ens', 'region')), parts along dimension 0, may hold values from -1 to 8191, as said below
- long_recv: int32 [16384], P(('ens', 'region')), parts along dimension 0, may hold values from 0 to 511
- long_geo: float32 [4, 16384], P(None, ('ens', 'region')), parts along dimension 1, may hold values from -6 to 6
- dec_send: int32 [3, 16384], P(None, ('ens', 'region')), parts along dimension 1, may hold values from 0 to 8191, as said below
- dec_geo: float32 [4, 3, 16384], P(None, None, ('ens', 'region')), parts along dimension 2, may hold values from -6 to 6
- w_send: bfloat16 [512, 512], replicated, may hold values from -0.25 to 0.25
- w_recv: bfloat16 [512, 512], replicated, may hold values from -0.25 to 0.25
- w_edge_geo: float32 [4, 512], replicated, may hold values from -3 to 3
- w_message: bfloat16 [512, 512], replicated, may hold values from -0.25 to 0.25
- w_node_self: bfloat16 [512, 512], replicated, may hold values from -0.25 to 0.25
- w_node_agg: bfloat16 [512, 512], replicated, may hold values from -0.25 to 0.25
- w_node_out: bfloat16 [512, 512], replicated, may hold values from -0.25 to 0.25
- w_dec_send: bfloat16 [512, 512], replicated, may hold values from -0.25 to 0.25
- w_dec_grid: bfloat16 [512, 512], replicated, may hold values from -0.25 to 0.25
- w_dec_geo: float32 [4, 512], replicated, may hold values from -3 to 3
- decoding_link_final_matrix: bfloat16 [512, 512], replicated, may hold values from -0.25 to 0.25
- w_grid_agg: bfloat16 [512, 512], replicated, may hold values from -0.25 to 0.25
- w_grid_self: bfloat16 [512, 512], replicated, may hold values from -0.25 to 0.25
- final_projection_matrix: bfloat16 [100, 512], replicated, may hold values from -0.25 to 0.25
Outputs:
- refreshed_mesh_latents: bfloat16 [16384, 512], P(('ens', 'region')), parts along dimension 0
- predicted_fields: bfloat16 [100, 16384], P(None, ('ens', 'region')), parts along dimension 1
There are 2 independent parts, one for each index of `ens`. A program takes and returns all parts, laid end to end along the dimension named above; an argument that names none is the same for every part. Nothing has to cross between parts.
Inputs may be any that keep to these rules, and one draw needn't show every extreme that they name: `fine_edge_sender`: A fine edge held by region d has its sender in region d, among the last 64 nodes of region d - 1, or among the first 64 nodes of region d + 1; node 448 of region d - 1 (the first of its last 64) and node 63 of region d + 1 are used where those regions exist. `long_send`: slot d * 512 + o * 32 + j, unless -1, names one of the first 64 nodes of region o; in every region one other region's 32 slots are all filled. `dec_send`: the senders of a grid point of band d lie in region d, among the last 64 nodes of region d - 1, or among the first 64 nodes of region d + 1; node 448 of region d - 1 (the first of its last 64) and node 63 of region d + 1 are used where those regions exist.
All inputs are finite; a program needn't handle non-finite values.
Results may differ from a plain program's by a relative error of at most 0.013.
Values may be sent and summed in bfloat16 or wider, within the bound.
A program may use at most 128 MiB of HBM per device.

v0:
```python
import jax
import jax.numpy as jnp
from jax import lax
from jax.sharding import PartitionSpec as P

BORDER = 64


def extended_2(array, sides, width):
    for axis, dim in sides:
        size, length = (lax.axis_size(axis), array.shape[dim])
        up = [(i, (i + 1) % size) for i in range(size - 1)]
        down = [(j, i) for i, j in up]
        last = lax.slice_in_dim(array, length - width, length, axis=dim)
        initial = lax.slice_in_dim(array, 0, width, axis=dim)
        before = lax.ppermute(last, axis, up)
        after = lax.ppermute(initial, axis, down)
        array = jnp.concatenate([before, array, after], axis=dim)
    return array


def product(left, right):
    return jnp.dot(left, right, preferred_element_type=jnp.float32)


def geometry(feature_vectors, learned_factor):
    return lax.dot_general(
        feature_vectors, learned_factor, (((0,), (0,)), ((), ())), precision=lax.Precision.HIGHEST
    )


def normalize(values):
    middle_point = values - jnp.mean(values, axis=-1, keepdims=True)
    spread = jnp.mean(middle_point * middle_point, axis=-1, keepdims=True)
    return middle_point * lax.rsqrt(spread + 1e-05)


def messages(edge_pre, w_message):
    edge_hidden = jax.nn.silu(edge_pre).astype(jnp.bfloat16)
    return normalize(product(edge_hidden, w_message))


def body(
    node_latent,
    grid_latent,
    fine_edge_sender,
    short_recv,
    short_geo,
    long_send,
    long_recv,
    long_geo,
    dec_send,
    dec_geo,
    w_send,
    w_recv,
    w_edge_geo,
    w_message,
    w_node_self,
    w_node_agg,
    w_node_out,
    w_dec_send,
    w_dec_grid,
    w_dec_geo,
    decoding_link_final_matrix,
    w_grid_agg,
    w_grid_self,
    final_projection_matrix,
):
    node_count = node_latent.shape[0]
    channel_count = node_latent.shape[1]
    region = lax.axis_index("region")
    row_offset = region * node_count - BORDER
    extended = extended_2(node_latent, (("region", 0),), BORDER)
    send_ext = product(extended, w_send)
    recv_proj = product(node_latent, w_recv)
    fine_pre = (
        send_ext[fine_edge_sender - row_offset]
        + recv_proj[short_recv]
        + geometry(short_geo, w_edge_geo)
    )
    fine_msg = messages(fine_pre, w_message)
    present = long_send >= 0
    clipped = jnp.maximum(long_send, 0)
    owner = clipped // node_count
    within = clipped - owner * node_count
    regions = lax.axis_size("region")
    asked = within.reshape(regions, -1)
    fetched = lax.all_to_all(
        node_latent[lax.all_to_all(asked, "region", split_axis=0, concat_axis=0, tiled=True)],
        "region",
        split_axis=0,
        concat_axis=0,
        tiled=True,
    ).reshape(-1, channel_count)
    far_pre = product(fetched, w_send) + recv_proj[long_recv] + geometry(long_geo, w_edge_geo)
    far_msg = messages(far_pre, w_message) * present[:, None].astype(jnp.float32)
    aggregate = (
        jnp.zeros((node_count, channel_count), jnp.float32)
        .at[short_recv]
        .add(fine_msg)
        .at[long_recv]
        .add(far_msg)
    )
    node_hidden = jax.nn.silu(
        product(node_latent, w_node_self) + product(aggregate.astype(jnp.bfloat16), w_node_agg)
    ).astype(jnp.bfloat16)
    refreshed_mesh_latents = (
        node_latent.astype(jnp.float32) + product(node_hidden, w_node_out)
    ).astype(jnp.bfloat16)
    updated_extended = extended_2(refreshed_mesh_latents, (("region", 0),), BORDER)
    dec_proj = product(updated_extended, w_dec_send)
    grid_proj = product(grid_latent, w_dec_grid)
    grid_sum = jnp.zeros(grid_proj.shape, jnp.float32)
    for vertex in range(3):
        dec_pre = (
            dec_proj[dec_send[vertex] - row_offset]
            + grid_proj
            + geometry(dec_geo[:, vertex, :], w_dec_geo)
        )
        grid_sum = grid_sum + messages(dec_pre, decoding_link_final_matrix)
    grid_agg = grid_sum.astype(jnp.bfloat16)
    latitude_site_latent_matrix = jax.nn.silu(
        product(grid_agg, w_grid_agg) + product(grid_latent, w_grid_self)
    ).astype(jnp.bfloat16)
    predicted_fields = lax.dot_general(
        final_projection_matrix,
        latitude_site_latent_matrix,
        (((1,), (1,)), ((), ())),
        preferred_element_type=jnp.float32,
    ).astype(jnp.bfloat16)
    return (refreshed_mesh_latents, predicted_fields)


def solution(mesh):
    in_specs = (
        P(("ens", "region"), None),
        P(("ens", "region"), None),
        P(("ens", "region")),
        P(("ens", "region")),
        P(None, ("ens", "region")),
        P(("ens", "region")),
        P(("ens", "region")),
        P(None, ("ens", "region")),
        P(None, ("ens", "region")),
        P(None, None, ("ens", "region")),
        P(),
        P(),
        P(),
        P(),
        P(),
        P(),
        P(),
        P(),
        P(),
        P(),
        P(),
        P(),
        P(),
        P(),
    )
    out_specs = (P(("ens", "region"), None), P(None, ("ens", "region")))
    return jax.shard_map(body, mesh=mesh, in_specs=in_specs, out_specs=out_specs, check_vma=False)
```

profile of v0, /device:TPU:1, one launch (start us, length us, event | category | flops | bytes accessed | tf_op | source)
XLA Modules:
  0.0 132.8 jit_solution(15853296209171749874)
XLA Ops:
  0.6 0.0 copy-start
  0.7 0.9 fusion.44
  1.6 4.5 %collective-permute-start = (bf16[64,512]{1,0:T(8,128)(2,1)S(1)}, bf16[64,512]{1,0:T(8,128)(2,1)S(1)}, u32[]{:S(2)}, u32[]{:S(2)}) collective-permute-start(bf16[64,512]{1,0:T(8,128)(2,1)S(1)} %get-tuple-element.4), channel_id=1, source_target_pairs={{0,1},{1,2},{2,3},{3,4},{4,5},{5,6},{6,7},{7,8},{8,9},{9,10},{10,1... | collective-permute-start | bytes 196616 | tf_op jit(solution)/shard_map/ppermute | solution.py:16
  6.2 1.9 %collective-permute-start.1 = (bf16[64,512]{1,0:T(8,128)(2,1)S(1)}, bf16[64,512]{1,0:T(8,128)(2,1)}, u32[]{:S(2)}, u32[]{:S(2)}) collective-permute-start(bf16[64,512]{1,0:T(8,128)(2,1)S(1)} %get-tuple-element.5), channel_id=1, source_target_pairs={{1,0},{2,1},{3,2},{4,3},{5,4},{6,5},{7,6},{8,7},{9,8},{10,9},{11,1... | collective-permute-start | bytes 196616 | tf_op jit(solution)/shard_map/ppermute | solution.py:17
  8.1 0.7 fusion.36
  8.8 0.7 all_to_all.11
  9.5 6.5 %all-to-all-start = ((s32[16,1,32]{2,1,0:T(1,128)}), s32[16,1,32]{2,1,0:T(1,128)S(1)}, u32[]{:S(2)}, u32[]{:S(2)}) async-start(s32[16,1,32]{2,1,0:T(1,128)} %all_to_all.11), calls=%async_computation | async-start | bytes 16384 | tf_op jit(solution)/shard_map/all_to_all | solution.py:89
  15.9 0.7 compare_convert_fusion
  16.6 1.7 %fusion.51 = f32[512,512]{1,0:T(8,128)S(1)} fusion(bf16[512,512]{1,0:T(8,128)(2,1)} %param.24, bf16[512,512]{1,0:T(8,128)(2,1)} %param.35), kind=kOutput, calls=%fused_computation.110 | convolution fusion | flops 268435456 | bytes 2097152 | tf_op jit(solution)/shard_map/dot_general | solution.py:23
  18.3 0.7 broadcast_clamp_fusion
  19.0 0.7 compare_select_fusion.6
  19.7 2.6 %fusion.50 = f32[512,512]{1,0:T(8,128)} fusion(bf16[512,512]{1,0:T(8,128)(2,1)} %param.24, bf16[512,512]{1,0:T(8,128)(2,1)} %param.38), kind=kOutput, calls=%fused_computation.109 | convolution fusion | flops 268435456 | bytes 2097152 | tf_op jit(solution)/shard_map/dot_general | solution.py:23
  22.4 0.0 copy-done.12
  22.4 5.0 %fusion.52 = f32[2048,512]{1,0:T(8,128)} fusion(f32[4,2048]{1,0:T(4,128)S(1)} %copy-done.8, f32[4,512]{1,0:T(4,128)S(1)} %copy-done.10), kind=kOutput, calls=%fused_computation.111 | convolution fusion | flops 50331648 | bytes 4235264 | tf_op jit(solution)/shard_map/dot_general | solution.py:27
  27.5 1.5 %fusion.53 = f32[512,512]{1,0:T(8,128)} fusion(bf16[512,512]{1,0:T(8,128)(2,1)S(1)} %copy-done.5, bf16[512,512]{1,0:T(8,128)(2,1)S(1)} %copy-done.4), kind=kOutput, calls=%fused_computation.112 | convolution fusion | flops 268435456 | bytes 2097152 | tf_op jit(solution)/shard_map/dot_general | solution.py:23
  29.0 8.9 %gather_fusion.1 = f32[2048,512]{1,0:T(8,128)} fusion(f32[512,512]{1,0:T(8,128)S(1)} %fusion.51, s32[2048]{0:T(1024)S(1)} %get-tuple-element.9), kind=kCustom, calls=%fused_computation.1 | custom fusion | bytes 8396800 | tf_op jit(solution)/shard_map/gather | solution.py:78
  37.9 1.6 %gather_fusion.3 = f32[512,512]{1,0:T(8,128)S(1)} fusion(f32[512,512]{1,0:T(8,128)S(1)} %fusion.51, s32[1024]{0:T(1024)S(1)} %pad_clamp_fusion.3), kind=kCustom, calls=%fused_computation.3 | custom fusion | bytes 2099200 | tf_op jit(solution)/shard_map/gather | solution.py:95
  39.5 0.0 all-to-all-done
  39.5 0.1 reshape.183
  39.6 2.6 %gather_fusion.2 = bf16[512,512]{1,0:T(8,128)(2,1)} fusion(bf16[512,512]{1,0:T(8,128)(2,1)S(1)} %copy-done.1, s32[1024]{0:T(1024)S(1)} %pad_clamp_fusion.4), kind=kCustom, calls=%fused_computation.2 | custom fusion | bytes 1050624 | tf_op jit(solution)/shard_map/gather | solution.py:89
  42.2 6.0 %all-to-all-start.1 = ((bf16[16,32,512]{2,1,0:T(8,128)(2,1)}), bf16[16,32,512]{2,1,0:T(8,128)(2,1)}, u32[]{:S(2)}, u32[]{:S(2)}) async-start(bf16[16,32,512]{2,1,0:T(8,128)(2,1)} %bitcast.1), calls=%async_computation.1 | async-start | bytes 1048576 | tf_op jit(solution)/shard_map/all_to_all | solution.py:88
  48.3 0.0 collective-permute-done
  48.3 0.0 collective-permute-done.1
  48.3 1.6 %fusion.3 = f32[640,512]{1,0:T(8,128)S(1)} fusion(bf16[512,512]{1,0:T(8,128)(2,1)} %param.34, bf16[64,512]{1,0:T(8,128)(2,1)} %collective-permute-done.1, bf16[512,512]{1,0:T(8,128)(2,1)S(1)} %copy-done.1, bf16[64,512]{1,0:T(8,128)(2,1)S(1)} %collective-permute-done), kind=kOutput, calls=%fused_computation.36 | convolution fusion | flops 337510400 | bytes 2490368 | tf_op jit(solution)/shard_map/dot_general | solution.py:23
  49.9 9.0 %gather_fusion = f32[2048,512]{1,0:T(8,128)} fusion(f32[640,512]{1,0:T(8,128)S(1)} %fusion.3, s32[2048]{0:T(1024)S(1)} %fusion.28), kind=kCustom, calls=%fused_computation | custom fusion | bytes 8396800 | tf_op jit(solution)/shard_map/gather | solution.py:77
  58.8 6.4 %fusion.45 = (f32[2048]{0:T(1024)S(1)}, f32[2048,512]{0,1:T(8,128)S(1)}) fusion(bf16[512,512]{1,0:T(8,128)(2,1)S(1)} %copy-done, f32[2048,512]{1,0:T(8,128)} %fusion.52, f32[2048,512]{1,0:T(8,128)} %gather_fusion, f32[2048,512]{1,0:T(8,128)} %gather_fusion.1), kind=kOutput, calls=%fused_computation.104 | convolution fusion | flops 1082128384 | bytes 17309696 | tf_op jit(solution)/shard_map/dot_general | solution.py:23
  65.3 0.5 multiply_reduce_fusion
  65.8 2.4 %subtract_multiply_fusion = f32[2048,512]{0,1:T(8,128)} fusion(f32[2048,512]{0,1:T(8,128)S(1)} %get-tuple-element.12, f32[2048]{0:T(1024)S(1)} %add_rsqrt_fusion, f32[2048]{0:T(1024)S(1)} %broadcast_multiply_fusion), kind=kLoop, calls=%fused_computation.11 | loop fusion | flops 2097152 | bytes 8404992 | tf_op jit(solution)/shard_map/mul | solution.py:35
  68.2 5.3 %copy.26 = f32[2048,512]{1,0:T(8,128)} copy(f32[2048,512]{0,1:T(8,128)} %subtract_multiply_fusion) | data formatting | bytes 8388608 | tf_op jit(solution)/shard_map/mul | solution.py:35
  73.6 13.7 %scatter_custom_fusion = f32[512,512]{1,0:T(8,128)S(1)} fusion(s32[2048]{0:T(1024)S(1)} %get-tuple-element.10, f32[2048,512]{1,0:T(8,128)} %copy.26, f32[]{:T(128)} %constant.51.clone.1), kind=kCustom, calls=%fused_computation.58 | custom fusion | flops 1048576 | bytes 1049088 | tf_op jit(solution)/shard_map/scatter-add | solution.py:100
  87.3 0.0 all-to-all-done.1
  87.3 1.6 %convolution_add_fusion.7 = f32[512,512]{1,0:T(8,128)S(1)} fusion(f32[512,512]{1,0:T(8,128)S(1)} %gather_fusion.3, bf16[512,512]{1,0:T(8,128)(2,1)} %bitcast.2, bf16[512,512]{1,0:T(8,128)(2,1)} %param.34), kind=kOutput, calls=%fused_computation.20 | convolution fusion | flops 268697600 | bytes 3145728 | tf_op jit(solution)/shard_map/dot_general | solution.py:23
  88.9 1.2 multiply_convert_fusion.7
  90.1 0.5 fusion.46
  90.6 0.2 multiply_reduce_fusion.4
  90.8 1.2 multiply_multiply_fusion
  92.0 1.6 %copy.27 = f32[512,512]{1,0:T(8,128)S(1)} copy(f32[512,512]{0,1:T(8,128)} %multiply_multiply_fusion) | data formatting | bytes 2097152 | tf_op jit(solution)/shard_map/mul | solution.py:96
  93.5 4.0 %scatter_fusion = f32[512,512]{1,0:T(8,128)S(1)} fusion(f32[512,512]{1,0:T(8,128)S(1)} %scatter_custom_fusion, s32[512]{0:T(512)S(1)} %compare_select_fusion.6, f32[512,512]{1,0:T(8,128)S(1)} %copy.27), kind=kCustom, calls=%fused_computation.8 | custom fusion | flops 262144 | bytes 3147776 | tf_op jit(solution)/shard_map/scatter-add | solution.py:102
  97.5 2.4 %fusion.1 = bf16[512,512]{1,0:T(8,128)(2,1)S(1)} fusion(bf16[512,512]{1,0:T(8,128)(2,1)} %param.40, f32[512,512]{1,0:T(8,128)} %fusion.50, bf16[512,512]{1,0:T(8,128)(2,1)} %param.39, bf16[512,512]{1,0:T(8,128)(2,1)S(1)} %copy-done.1, f32[512,512]{1,0:T(8,128)S(1)} %scatter_fusion), kind=kOutput, calls=%fused_computation.21 | convolution fusion | flops 539492352 | bytes 4194304 | tf_op jit(solution)/shard_map/dot_general | solution.py:23
  99.9 0.0 copy-start.9
  99.9 3.5 %collective-permute-start.2 = (bf16[64,512]{1,0:T(8,128)(2,1)S(1)}, bf16[64,512]{1,0:T(8,128)(2,1)S(1)}, u32[]{:S(2)}, u32[]{:S(2)}) collective-permute-start(bf16[64,512]{1,0:T(8,128)(2,1)S(1)} %get-tuple-element.2), channel_id=1, source_target_pairs={{0,1},{1,2},{2,3},{3,4},{4,5},{5,6},{6,7},{7,8},{8,9},{9,10},{10,1... | collective-permute-start | bytes 196616 | tf_op jit(solution)/shard_map/ppermute | solution.py:16
  103.5 1.9 %collective-permute-start.3 = (bf16[64,512]{1,0:T(8,128)(2,1)S(1)}, bf16[64,512]{1,0:T(8,128)(2,1)S(1)}, u32[]{:S(2)}, u32[]{:S(2)}) collective-permute-start(bf16[64,512]{1,0:T(8,128)(2,1)S(1)} %get-tuple-element.3), channel_id=1, source_target_pairs={{1,0},{2,1},{3,2},{4,3},{5,4},{6,5},{7,6},{8,7},{9,8},{10,9},{11,1... | collective-permute-start | bytes 196616 | tf_op jit(solution)/shard_map/ppermute | solution.py:17
  105.4 0.0 collective-permute-done.2
  105.4 3.6 %collective-permute-done.3 = bf16[64,512]{1,0:T(8,128)(2,1)S(1)} collective-permute-done((bf16[64,512]{1,0:T(8,128)(2,1)S(1)}, bf16[64,512]{1,0:T(8,128)(2,1)S(1)}, u32[]{:S(2)}, u32[]{:S(2)}) %collective-permute-start.3) | collective-permute-done | bytes 65568 | tf_op jit(solution)/shard_map/ppermute | solution.py:17
  109.1 1.5 %fusion.9 = f32[640,512]{1,0:T(8,128)S(1)} fusion(bf16[512,512]{1,0:T(8,128)(2,1)} %param.41, bf16[64,512]{1,0:T(8,128)(2,1)S(1)} %collective-permute-done.3, bf16[512,512]{1,0:T(8,128)(2,1)S(1)} %fusion.1, bf16[64,512]{1,0:T(8,128)(2,1)S(1)} %collective-permute-done.2), kind=kOutput, calls=%fused_computation.42 | convolution fusion | flops 337510400 | bytes 2490368 | tf_op jit(solution)/shard_map/dot_general | solution.py:23
  110.6 0.0 copy-start.14
  110.6 0.0 copy-start.16
  110.6 1.6 %gather_fusion.4 = f32[512,512]{1,0:T(8,128)S(1)} fusion(f32[640,512]{1,0:T(8,128)S(1)} %fusion.9, s32[1024]{0:T(1024)S(1)} %pad_clamp_fusion.2), kind=kCustom, calls=%fused_computation.4 | custom fusion | bytes 2099200 | tf_op jit(solution)/shard_map/gather | solution.py:116
  112.3 0.0 copy-start.3
  112.3 2.5 %multiply_convert_fusion.5 = bf16[512,512]{1,0:T(8,128)(2,1)S(1)} fusion(f32[4,512]{1,0:T(4,128)S(1)} %copy-done.16, f32[512,512]{1,0:T(8,128)S(1)} %gather_fusion.4, f32[512,512]{1,0:T(8,128)} %fusion.53, f32[4,3,512]{2,0,1:T(4,128)S(1)} %copy-done.14), kind=kOutput, calls=%fused_computation.31 | convolution fusion | flops 14417920 | bytes 2637824 | tf_op jit(solution)/shard_map/dot_general | solution.py:27
  114.8 0.5 fusion.49
  115.3 0.2 multiply_reduce_fusion.3
  115.5 2.3 %gather_fusion.5 = f32[512,512]{1,0:T(8,128)} fusion(f32[640,512]{1,0:T(8,128)S(1)} %fusion.9, s32[1024]{0:T(1024)S(1)} %pad_clamp_fusion.1), kind=kCustom, calls=%fused_computation.5 | custom fusion | bytes 2099200 | tf_op jit(solution)/shard_map/gather | solution.py:116
  117.9 2.8 %multiply_convert_fusion.4 = bf16[512,512]{1,0:T(8,128)(2,1)S(1)} fusion(f32[4,512]{1,0:T(4,128)S(1)} %copy-done.16, f32[512,512]{1,0:T(8,128)} %gather_fusion.5, f32[512,512]{1,0:T(8,128)} %fusion.53, f32[4,3,512]{2,0,1:T(4,128)S(1)} %copy-done.14), kind=kOutput, calls=%fused_computation.29 | convolution fusion | flops 14417920 | bytes 2637824 | tf_op jit(solution)/shard_map/dot_general | solution.py:27
  120.6 1.5 %fusion.48 = (f32[512]{0:T(512)S(1)}, f32[512,512]{0,1:T(8,128)}) fusion(bf16[512,512]{1,0:T(8,128)(2,1)S(1)} %multiply_convert_fusion.4, bf16[512,512]{1,0:T(8,128)(2,1)S(1)} %copy-done.3), kind=kOutput, calls=%fused_computation.107 | convolution fusion | flops 268697088 | bytes 2099200 | tf_op jit(solution)/shard_map/dot_general | solution.py:23
  122.1 2.3 %gather_fusion.6 = f32[512,512]{1,0:T(8,128)} fusion(f32[640,512]{1,0:T(8,128)S(1)} %fusion.9, s32[1024]{0:T(1024)S(1)} %pad_clamp_fusion), kind=kCustom, calls=%fused_computation.6 | custom fusion | bytes 2099200 | tf_op jit(solution)/shard_map/gather | solution.py:116
  124.4 2.9 %multiply_convert_fusion.3 = bf16[512,512]{1,0:T(8,128)(2,1)S(1)} fusion(f32[4,512]{1,0:T(4,128)S(1)} %copy-done.16, f32[512,512]{1,0:T(8,128)} %gather_fusion.6, f32[512,512]{1,0:T(8,128)} %fusion.53, f32[4,3,512]{2,0,1:T(4,128)S(1)} %copy-done.14), kind=kOutput, calls=%fused_computation.27 | convolution fusion | flops 14417920 | bytes 2637824 | tf_op jit(solution)/shard_map/dot_general | solution.py:27
  127.3 0.0 copy-start.13
  127.3 0.5 fusion.47
  127.8 0.0 copy-start.6
  127.9 0.2 multiply_reduce_fusion.2
  128.0 0.2 multiply_reduce_fusion.1
  128.2 1.7 %fusion.15 = f32[512,512]{1,0:T(8,128)} fusion(bf16[512,512]{1,0:T(8,128)(2,1)S(1)} %copy-done.7, f32[512,512]{0,1:T(8,128)S(1)} %get-tuple-element.16, f32[512,512]{0,1:T(8,128)S(1)} %copy-done.2, f32[512,512]{0,1:T(8,128)S(1)} %get-tuple-element.20, f32[512]{0:T(512)S(1)} %get-tuple-element.21, f32[512]{0:T(512)S(1)} %broadcast_multiply_fusion.1, ...), kind=kOutput, calls=%fused_computation.48 | convolution fusion | flops 270794752 | bytes 4730880 | tf_op jit(solution)/shard_map/dot_general | solution.py:23
  129.9 2.8 %fusion.2 = bf16[100,512]{1,0:T(8,128)(2,1)} fusion(bf16[100,512]{1,0:T(8,128)(2,1)S(1)} %copy-done.13, f32[512,512]{1,0:T(8,128)} %fusion.15, bf16[512,512]{1,0:T(8,128)(2,1)S(1)} %copy-done.6, bf16[512,512]{1,0:T(8,128)(2,1)} %param.46), kind=kOutput, calls=%fused_computation.23 | convolution fusion | flops 322488320 | bytes 2301952 | tf_op jit(solution)/shard_map/dot_general | solution.py:125
  (44 shorter events, 0.2 us)
Async XLA Ops:
  0.6 58.2 %copy-start = (bf16[512,512]{1,0:T(8,128)(2,1)S(1)}, bf16[512,512]{1,0:T(8,128)(2,1)}, u32[]{:S(2)}) copy-start(bf16[512,512]{1,0:T(8,128)(2,1)} %param.37) | copy-start | bytes 1572868
  0.6 21.7 %copy-start.11 = (s32[2048]{0:T(1024)S(1)}, s32[2048]{0:T(1024)}, u32[]{:S(2)}) copy-start(s32[2048]{0:T(1024)} %param.26) | copy-start | bytes 24580
  0.7 21.7 %copy-start.12 = (s32[3,512]{1,0:T(4,128)S(1)}, s32[3,512]{1,0:T(4,128)}, u32[]{:S(2)}) copy-start(s32[3,512]{1,0:T(4,128)} %param.32) | copy-start | bytes 18436
  0.7 21.7 %copy-start.8 = (f32[4,2048]{1,0:T(4,128)S(1)}, f32[4,2048]{1,0:T(4,128)}, u32[]{:S(2)}) copy-start(f32[4,2048]{1,0:T(4,128)} %param.28) | copy-start | bytes 98308
  0.7 21.7 %copy-start.10 = (f32[4,512]{1,0:T(4,128)S(1)}, f32[4,512]{1,0:T(4,128)}, u32[]{:S(2)}) copy-start(f32[4,512]{1,0:T(4,128)} %param.36) | copy-start | bytes 24580
  1.6 46.6 %collective-permute-start = (bf16[64,512]{1,0:T(8,128)(2,1)S(1)}, bf16[64,512]{1,0:T(8,128)(2,1)S(1)}, u32[]{:S(2)}, u32[]{:S(2)}) collective-permute-start(bf16[64,512]{1,0:T(8,128)(2,1)S(1)} %get-tuple-element.4), channel_id=1, source_target_pairs={{0,1},{1,2},{2,3},{3,4},{4,5},{5,6},{6,7},{7,8},{8,9},{9,10},{10,1... | collective-permute-start | bytes 196616 | tf_op jit(solution)/shard_map/ppermute | solution.py:16
  6.2 42.1 %collective-permute-start.1 = (bf16[64,512]{1,0:T(8,128)(2,1)S(1)}, bf16[64,512]{1,0:T(8,128)(2,1)}, u32[]{:S(2)}, u32[]{:S(2)}) collective-permute-start(bf16[64,512]{1,0:T(8,128)(2,1)S(1)} %get-tuple-element.5), channel_id=1, source_target_pairs={{1,0},{2,1},{3,2},{4,3},{5,4},{6,5},{7,6},{8,7},{9,8},{10,9},{11,1... | collective-permute-start | bytes 196616 | tf_op jit(solution)/shard_map/ppermute | solution.py:17
  9.5 30.0 %all-to-all-start = ((s32[16,1,32]{2,1,0:T(1,128)}), s32[16,1,32]{2,1,0:T(1,128)S(1)}, u32[]{:S(2)}, u32[]{:S(2)}) async-start(s32[16,1,32]{2,1,0:T(1,128)} %all_to_all.11), calls=%async_computation | async-start | bytes 16384 | tf_op jit(solution)/shard_map/all_to_all | solution.py:89
  16.6 10.9 %copy-start.4 = (bf16[512,512]{1,0:T(8,128)(2,1)S(1)}, bf16[512,512]{1,0:T(8,128)(2,1)}, u32[]{:S(2)}) copy-start(bf16[512,512]{1,0:T(8,128)(2,1)} %param.42) | copy-start | bytes 1572868
  16.6 10.9 %copy-start.5 = (bf16[512,512]{1,0:T(8,128)(2,1)S(1)}, bf16[512,512]{1,0:T(8,128)(2,1)}, u32[]{:S(2)}) copy-start(bf16[512,512]{1,0:T(8,128)(2,1)} %param.25) | copy-start | bytes 1572868
  37.9 1.7 %copy-start.1 = (bf16[512,512]{1,0:T(8,128)(2,1)S(1)}, bf16[512,512]{1,0:T(8,128)(2,1)}, u32[]{:S(2)}) copy-start(bf16[512,512]{1,0:T(8,128)(2,1)} %param.24) | copy-start | bytes 1572868
  42.2 45.0 %all-to-all-start.1 = ((bf16[16,32,512]{2,1,0:T(8,128)(2,1)}), bf16[16,32,512]{2,1,0:T(8,128)(2,1)}, u32[]{:S(2)}, u32[]{:S(2)}) async-start(bf16[16,32,512]{2,1,0:T(8,128)(2,1)} %bitcast.1), calls=%async_computation.1 | async-start | bytes 1048576 | tf_op jit(solution)/shard_map/all_to_all | solution.py:88
  73.6 15.3 %copy-start.15 = (f32[4,512]{1,0:T(4,128)S(1)}, f32[4,512]{1,0:T(4,128)}, u32[]{:S(2)}) copy-start(f32[4,512]{1,0:T(4,128)} %param.31) | copy-start | bytes 24580
  99.9 9.2 %copy-start.9 = (bf16[512,512]{1,0:T(8,128)(2,1)}, bf16[512,512]{1,0:T(8,128)(2,1)S(1)}, u32[]{:S(2)}) copy-start(bf16[512,512]{1,0:T(8,128)(2,1)S(1)} %fusion.1) | copy-start | bytes 1572868
  99.9 5.5 %collective-permute-start.2 = (bf16[64,512]{1,0:T(8,128)(2,1)S(1)}, bf16[64,512]{1,0:T(8,128)(2,1)S(1)}, u32[]{:S(2)}, u32[]{:S(2)}) collective-permute-start(bf16[64,512]{1,0:T(8,128)(2,1)S(1)} %get-tuple-element.2), channel_id=1, source_target_pairs={{0,1},{1,2},{2,3},{3,4},{4,5},{5,6},{6,7},{7,8},{8,9},{9,10},{10,1... | collective-permute-start | bytes 196616 | tf_op jit(solution)/shard_map/ppermute | solution.py:16
  103.5 5.6 %collective-permute-start.3 = (bf16[64,512]{1,0:T(8,128)(2,1)S(1)}, bf16[64,512]{1,0:T(8,128)(2,1)S(1)}, u32[]{:S(2)}, u32[]{:S(2)}) collective-permute-start(bf16[64,512]{1,0:T(8,128)(2,1)S(1)} %get-tuple-element.3), channel_id=1, source_target_pairs={{1,0},{2,1},{3,2},{4,3},{5,4},{6,5},{7,6},{8,7},{9,8},{10,9},{11,1... | collective-permute-start | bytes 196616 | tf_op jit(solution)/shard_map/ppermute | solution.py:17
  110.6 1.7 %copy-start.14 = (f32[4,3,512]{2,0,1:T(4,128)S(1)}, f32[4,3,512]{2,0,1:T(4,128)}, u32[]{:S(2)}) copy-start(f32[4,3,512]{2,0,1:T(4,128)} %param.33) | copy-start | bytes 73732
  110.6 1.7 %copy-start.16 = (f32[4,512]{1,0:T(4,128)S(1)}, f32[4,512]{1,0:T(4,128)}, u32[]{:S(2)}) copy-start(f32[4,512]{1,0:T(4,128)} %param.43) | copy-start | bytes 24580
  112.3 2.5 %copy-start.3 = (bf16[512,512]{1,0:T(8,128)(2,1)S(1)}, bf16[512,512]{1,0:T(8,128)(2,1)}, u32[]{:S(2)}) copy-start(bf16[512,512]{1,0:T(8,128)(2,1)} %param.44) | copy-start | bytes 1572868
  124.4 3.4 %copy-start.2 = (f32[512,512]{0,1:T(8,128)S(1)}, f32[512,512]{0,1:T(8,128)}, u32[]{:S(2)}) copy-start(f32[512,512]{0,1:T(8,128)} %get-tuple-element.18) | copy-start | bytes 3145732
  124.4 3.8 %copy-start.7 = (bf16[512,512]{1,0:T(8,128)(2,1)S(1)}, bf16[512,512]{1,0:T(8,128)(2,1)}, u32[]{:S(2)}) copy-start(bf16[512,512]{1,0:T(8,128)(2,1)} %param.45) | copy-start | bytes 1572868
  127.3 2.6 %copy-start.13 = (bf16[100,512]{1,0:T(8,128)(2,1)S(1)}, bf16[100,512]{1,0:T(8,128)(2,1)}, u32[]{:S(2)}) copy-start(bf16[100,512]{1,0:T(8,128)(2,1)} %param.47) | copy-start | bytes 307204
  127.8 2.1 %copy-start.6 = (bf16[512,512]{1,0:T(8,128)(2,1)S(1)}, bf16[512,512]{1,0:T(8,128)(2,1)}, u32[]{:S(2)}) copy-start(bf16[512,512]{1,0:T(8,128)(2,1)} %param.25) | copy-start | bytes 1572868
where the time goes:
time: 134 us; the launch traced here: 133 us
  matrix products  41.2 us (31%)
  local copies, waits for them, and re-layouts  37.1 us (28%)
  other arithmetic  25.4 us (19%)
  starting transfers between devices  24.4 us (18%)
  waiting for transfers between devices  3.65 us (3%)
    dot_general x13, matrix products, product(): return jnp.dot(left, right, preferred_element_type=jnp.float32)  24 us
    scatter-add x2, other arithmetic, body(): aggregate = jnp.zeros((node_count, channel_count), jnp.float32).at[short_...  17.7 us
    dot_general x5, matrix products, geometry(): lax.dot_general(feature_vectors, learned_factor, (((0,), (0,)), ((), ()))...  14.3 us
    gather x1, local copies, waits for them, and re-layouts, body(): send_ext[fine_edge_sender - row_offset] + recv_proj[short_recv]  8.95 us
    gather x1, local copies, waits for them, and re-layouts, body(): recv_proj[short_recv]  8.91 us
    ppermute x2, starting transfers between devices, extended_2(): before = lax.ppermute(last, axis, up)  8.08 us
    all_to_all x1, starting transfers between devices, body(): lax.all_to_all(asked, 'region', split_axis=0, concat_axis=0, tiled=True)  6.45 us
    gather x3, local copies, waits for them, and re-layouts, body(): dec_proj[dec_send[vertex] - row_offset] + grid_proj  6.3 us
  transfers between devices with their start and end apart: 6, of which 1 were waited for; matrix products, arithmetic and copies ran while one was open for 50% of the time, Pallas kernels for 0%

commit v1 on v0

v1 whole, which is shorter than its diff:
```python
import functools

import jax
import jax.numpy as jnp
from jax import lax
from jax.experimental import pallas as pl
from jax.experimental.pallas import tpu as pltpu
from jax.sharding import PartitionSpec as P

BORDER = 64
COARSE = 64
TAIL = 128
LANES = 128
CHUNK = 512
F32 = jnp.float32
BF16 = jnp.bfloat16
MESH = pl.DeviceIdType.MESH


def dot(left, right):
    return jnp.dot(left, right, preferred_element_type=F32)


def silu(value):
    half = 0.5 * value
    return half + half * jnp.tanh(half)


def normalize(values):
    width = 1.0 / values.shape[-1]
    centred = values - jnp.sum(values, axis=-1, keepdims=True) * width
    spread = jnp.sum(centred * centred, axis=-1, keepdims=True) * width
    return centred * lax.rsqrt(spread + 1e-5)


def one_hot(place, count):
    lanes = lax.broadcasted_iota(jnp.int32, (place.shape[0], count), 1)
    return jnp.where(lanes == place, 1.0, 0.0).astype(BF16)


def one_hot_rows(place, count):
    rows = lax.broadcasted_iota(jnp.int32, (count, place.shape[1]), 0)
    return jnp.where(rows == place, 1.0, 0.0).astype(BF16)


def turn(slab):
    parts = []
    for start in range(0, slab.shape[1], LANES):
        piece = slab[:, start : start + LANES]
        full = jnp.concatenate([piece, jnp.zeros((LANES - 16, LANES), F32)], axis=0)
        parts.append(full.T)
    return jnp.concatenate(parts, axis=0)


def put_geometry(slab, geo):
    high = geo.astype(BF16).astype(F32)
    slab[4:8, :] = high
    slab[8:12, :] = geo - high
    slab[12:16, :] = high


def put_tail(table, start, w_geo):
    high = w_geo.astype(BF16).astype(F32)
    width = w_geo.shape[1]
    rows = jnp.concatenate(
        [jnp.zeros((4, width), F32), high, high, w_geo - high, jnp.zeros((TAIL - 16, width), F32)],
        axis=0,
    )
    table[start : start + TAIL, :] = rows.astype(BF16)


def kernel(
    regions,
    node,
    grid_hbm,
    fine_send,
    fine_recv,
    fine_geo,
    long_send,
    long_recv,
    long_geo,
    dec_send,
    dec_geo,
    w_send,
    w_recv,
    w_edge_geo,
    w_dec_geo,
    w_message_hbm,
    w_node_self_hbm,
    w_node_agg_hbm,
    w_node_out_hbm,
    w_dec_send_hbm,
    w_dec_grid_hbm,
    w_dec_final_hbm,
    w_grid_agg_hbm,
    w_grid_self_hbm,
    w_final_hbm,
    out_mesh,
    out_fields,
    grid,
    w_message,
    w_node_self,
    w_node_agg,
    w_node_out,
    w_dec_send,
    w_dec_grid,
    w_dec_final,
    w_grid_agg,
    w_grid_self,
    w_final,
    load_sem,
    edge_in,
    ends_out,
    ends_in,
    border_send,
    border_recv,
    coarse,
    z_send,
    z_recv,
    y_send,
    y_recv,
    c_send,
    c_recv,
    table,
    coarse_table,
    dec_table,
    slab_fine,
    slab_long,
    slab_dec,
    total,
    self_part,
    grid_part,
    grid_own,
):
    nodes, width = node.shape
    edges = slab_fine.shape[1]
    slots = slab_long.shape[1]
    points = slab_dec.shape[2]
    span = nodes + 2 * BORDER
    ens = lax.axis_index("ens")
    me = lax.axis_index("region")
    line = regions // 4
    spot = me // 4
    lane = me % 4
    twin = me + 1 - 2 * (me % 2)
    side = lane % 4
    across = me + 2 - 4 * (side // 2)

    loads = [
        (grid_hbm, grid),
        (w_message_hbm, w_message),
        (w_node_self_hbm, w_node_self),
        (w_node_agg_hbm, w_node_agg),
        (w_node_out_hbm, w_node_out),
        (w_dec_send_hbm, w_dec_send),
        (w_dec_grid_hbm, w_dec_grid),
        (w_dec_final_hbm, w_dec_final),
        (w_grid_agg_hbm, w_grid_agg),
        (w_grid_self_hbm, w_grid_self),
        (w_final_hbm, w_final),
    ]

    def load(number):
        return pltpu.make_async_copy(*loads[number], load_sem.at[number])

    for number in (1, 2, 0, 3, 4, 5, 6, 7, 8, 9, 10):
        load(number).start()

    has_left, has_right = me > 0, me < regions - 1
    has_back, has_next = spot > 0, spot < line - 1

    barrier = pltpu.get_barrier_semaphore()

    def greet(other):
        pl.semaphore_signal(barrier, inc=1, device_id=(ens, other), device_id_type=MESH)

    greet(across)
    for present, other in (
        (has_left, me - 1),
        (has_right, me + 1),
        (has_back, me - 4),
        (has_next, me + 4),
    ):
        pl.when(present)(functools.partial(greet, other))
    coarse[me] = node[:COARSE, :]
    count = 1
    for present in (has_left, has_right, has_back, has_next):
        count = count + present.astype(jnp.int32)
    pl.semaphore_wait(barrier, count)

    def remote(src, dst, send, recv, other):
        return pltpu.make_async_remote_copy(
            src_ref=src,
            dst_ref=dst,
            send_sem=send,
            recv_sem=recv,
            device_id=(ens, other),
            device_id_type=MESH,
        )

    def border_up(src, phase, into):
        return remote(
            src, into.at[0], border_send.at[phase, 0], border_recv.at[phase, 0], me + 1
        )

    def border_down(src, phase, into):
        return remote(
            src, into.at[1], border_send.at[phase, 1], border_recv.at[phase, 1], me - 1
        )

    def exchange(first, last, phase, into):
        pl.when(has_right)(lambda: border_up(last, phase, into).start())
        pl.when(has_left)(lambda: border_down(first, phase, into).start())

        @pl.when(jnp.logical_not(has_left))
        def _():
            into[0] = jnp.zeros((BORDER, width), BF16)

        @pl.when(jnp.logical_not(has_right))
        def _():
            into[1] = jnp.zeros((BORDER, width), BF16)

    def settle(first, last, phase, into):
        @pl.when(has_right)
        def _():
            border_up(last, phase, into).wait_send()
            border_down(first, phase, into).wait_recv()

        @pl.when(has_left)
        def _():
            border_down(first, phase, into).wait_send()
            border_up(last, phase, into).wait_recv()

    node_first, node_last = node.at[pl.ds(0, BORDER)], node.at[pl.ds(nodes - BORDER, BORDER)]
    exchange(node_first, node_last, 0, edge_in)

    def z_copy(way, step, place):
        block = coarse.at[place * 4 + lane]
        other = me + 4 - 8 * way
        return remote(block, block, z_send.at[way, step], z_recv.at[way, step], other)

    def y_copy(place):
        block = coarse.at[place * 4 + lane]
        return remote(block, block, y_send.at[place], y_recv.at[place], across)

    def c_copy(half, place):
        block = coarse.at[place * 4 + (lane + 2 * half) % 4]
        return remote(block, block, c_send.at[half, place], c_recv.at[half, place], twin)

    def spread(place):
        y_copy(place).start()
        c_copy(0, place).start()

    def step_z(step):
        for way in range(2):
            place = spot - step if way == 0 else spot + step
            held = (place >= 0) & (place < line)

            @pl.when(held)
            def _():
                if step > 0:
                    z_copy(way, step - 1, place).wait_recv()
                if step < line - 1:
                    onward = has_next if way == 0 else has_back
                    pl.when(onward)(lambda: z_copy(way, step, place).start())
                if step > 0 or way == 0:
                    spread(place)

    def step_y():
        for place in range(line):
            y_copy(place).wait_recv()
            c_copy(1, place).start()

    def step_end():
        for place in range(line):
            for half in range(2):
                c_copy(half, place).wait()
            y_copy(place).wait_send()
        for step in range(line - 1):
            for way in range(2):
                place = spot - step if way == 0 else spot + step
                onward = has_next if way == 0 else has_back
                held = (place >= 0) & (place < line) & onward
                pl.when(held)(lambda: z_copy(way, step, place).wait_send())

    step_z(0)

    own = node[...]
    table[BORDER : BORDER + nodes, :] = dot(own, w_send[...]).astype(BF16)
    table[span : span + nodes, :] = dot(own, w_recv[...]).astype(BF16)
    put_tail(table, span + nodes, w_edge_geo[...])
    put_tail(dec_table, span, w_dec_geo[...])
    offset = me * nodes - BORDER
    for slab, geo in ((slab_fine, fine_geo[...]), (slab_long, long_geo[...])):
        put_geometry(slab, geo)
        slab[2:4, :] = jnp.zeros((2, geo.shape[1]), F32)
    for row in range(edges // LANES):
        at = pl.ds(row * LANES, LANES)
        slab_fine[0:1, at] = (fine_send[row : row + 1, :] - offset).astype(F32)
        slab_fine[1:2, at] = fine_recv[row : row + 1, :].astype(F32)
    per_owner = slots // regions
    group = max(per_owner, slots // 2)
    owners = group // per_owner
    for row in range(slots // LANES):
        at = pl.ds(row * LANES, LANES)
        slot = lax.broadcasted_iota(jnp.int32, (1, LANES), 1) + row * LANES
        owner = slot // per_owner
        sender = long_send[row : row + 1, :]
        base = (row * LANES // group) * owners
        within = sender - owner * nodes + (owner - base) * COARSE
        full = sender >= 0
        slab_long[0:1, at] = jnp.where(full, within, -1).astype(F32)
        slab_long[1:2, at] = jnp.where(full, long_recv[row : row + 1, :], -1).astype(F32)
    for k in range(3):
        slab_dec[k, 0:1, :] = (dec_send[k : k + 1, :] - offset).astype(F32)
        slab_dec[k, 1:4, :] = jnp.zeros((3, points), F32)
        for i in range(4):
            geo = dec_geo[i, k : k + 1, :]
            high = geo.astype(BF16).astype(F32)
            slab_dec[k, 4 + i : 5 + i, :] = high
            slab_dec[k, 8 + i : 9 + i, :] = geo - high
            slab_dec[k, 12 + i : 13 + i, :] = high
    total[...] = jnp.zeros(total.shape, F32)
    load(2).wait()
    self_part[...] = dot(own, w_node_self[...])
    load(1).wait()

    settle(node_first, node_last, 0, edge_in)
    border = jnp.concatenate([edge_in[0], edge_in[1]], axis=0)
    border_proj = dot(border, w_send[...]).astype(BF16)
    table[0:BORDER, :] = border_proj[:BORDER]
    table[BORDER + nodes : span, :] = border_proj[BORDER:]

    def add_messages(pre, slab_rows):
        message = normalize(dot(silu(pre).astype(BF16), w_message[...])).astype(BF16)
        total[...] += dot(one_hot_rows(slab_rows.astype(jnp.int32), nodes), message)

    loops = edges // CHUNK
    steps = [functools.partial(step_z, step) for step in range(1, line)] + [step_y]
    turns = [[] for _ in range(loops)]
    for number, step in enumerate(steps):
        turns[number * loops // len(steps)].append(step)

    def fine(i, carry):
        for number, group_of in enumerate(turns):
            if group_of:

                @pl.when(i == number)
                def _():
                    for step in group_of:
                        step()

        at = pl.ds(pl.multiple_of(i * CHUNK, CHUNK), CHUNK)
        slab = slab_fine[:, at]
        turned = turn(slab)
        place = turned[:, 0:2].astype(jnp.int32)
        pick = jnp.concatenate(
            [one_hot(place[:, 0:1], span), one_hot(place[:, 1:2], nodes), turned.astype(BF16)],
            axis=1,
        )
        add_messages(dot(pick, table[...]), slab[1:2, :])
        return carry

    lax.fori_loop(0, loops, fine, 0)

    step_end()
    coarse_table[...] = dot(
        coarse[...].reshape(regions * COARSE, width), w_send[...]
    ).astype(BF16)
    reach = owners * COARSE
    for number in range(slots // group):
        slab = slab_long[:, number * group : (number + 1) * group]
        turned = turn(slab)
        place = turned[:, 0:2].astype(jnp.int32)
        near = jnp.concatenate([one_hot(place[:, 1:2], nodes), turned.astype(BF16)], axis=1)
        pre = dot(
            one_hot(place[:, 0:1], reach), coarse_table[number * reach : (number + 1) * reach, :]
        ) + dot(near, table[span:, :])
        add_messages(pre, slab[1:2, :])

    load(3).wait()
    load(4).wait()

    def refresh(aggregate, own_part, latent):
        hidden = silu(own_part + dot(aggregate.astype(BF16), w_node_agg[...])).astype(BF16)
        return (latent.astype(F32) + dot(hidden, w_node_out[...])).astype(BF16)

    def both(ref):
        return jnp.concatenate([ref[:BORDER, :], ref[nodes - BORDER :, :]], axis=0)

    ends = refresh(both(total), both(self_part), both(node))
    ends_out[0] = ends[:BORDER]
    ends_out[1] = ends[BORDER:]
    exchange(ends_out.at[0], ends_out.at[1], 1, ends_in)
    inner = slice(BORDER, nodes - BORDER)
    out_mesh[inner, :] = refresh(total[inner, :], self_part[inner, :], node[inner, :])
    out_mesh[:BORDER, :] = ends[:BORDER]
    out_mesh[nodes - BORDER :, :] = ends[BORDER:]
    for number in (5, 0, 6, 9):
        load(number).wait()
    dec_table[BORDER : BORDER + nodes, :] = dot(out_mesh[...], w_dec_send[...]).astype(BF16)
    grid_part[...] = dot(grid[...], w_dec_grid[...])
    grid_own[...] = dot(grid[...], w_grid_self[...])
    for number in (7, 8, 10):
        load(number).wait()
    settle(ends_out.at[0], ends_out.at[1], 1, ends_in)
    border = jnp.concatenate([ends_in[0], ends_in[1]], axis=0)
    border_proj = dot(border, w_dec_send[...]).astype(BF16)
    dec_table[0:BORDER, :] = border_proj[:BORDER]
    dec_table[BORDER + nodes : span, :] = border_proj[BORDER:]

    part = points // 2

    for number in range(2):
        at = pl.ds(number * part, part)
        picks = []
        for k in range(3):
            turned = turn(slab_dec[k, :, at])
            place = turned[:, 0:1].astype(jnp.int32)
            picks.append(jnp.concatenate([one_hot(place, span), turned.astype(BF16)], axis=1))
        pick = jnp.concatenate(picks, axis=0)
        grid_three = jnp.concatenate([grid_part[at, :]] * 3, axis=0)
        pre = dot(pick, dec_table[...]) + grid_three
        message = normalize(dot(silu(pre).astype(BF16), w_dec_final[...]))
        gathered = message[:part] + message[part : 2 * part] + message[2 * part :]
        hidden = silu(dot(gathered.astype(BF16), w_grid_agg[...]) + grid_own[at, :])
        fields = lax.dot_general(
            w_final[...],
            hidden.astype(BF16),
            (((1,), (1,)), ((), ())),
            preferred_element_type=F32,
        )
        out_fields[:, at] = fields.astype(BF16)


def body(
    node_latent,
    grid_latent,
    fine_edge_sender,
    short_recv,
    short_geo,
    long_send,
    long_recv,
    long_geo,
    dec_send,
    dec_geo,
    w_send,
    w_recv,
    w_edge_geo,
    w_message,
    w_node_self,
    w_node_agg,
    w_node_out,
    w_dec_send,
    w_dec_grid,
    w_dec_geo,
    decoding_link_final_matrix,
    w_grid_agg,
    w_grid_self,
    final_projection_matrix,
):
    regions = lax.axis_size("region")
    nodes, width = node_latent.shape
    points = grid_latent.shape[0]
    edges, slots = fine_edge_sender.shape[0], long_send.shape[0]
    line = regions // 4
    fields = final_projection_matrix.shape[0]
    span = nodes + 2 * BORDER
    square = pltpu.VMEM((width, width), BF16)
    vmem = pl.BlockSpec(memory_space=pltpu.VMEM)
    anywhere = pl.BlockSpec(memory_space=pl.ANY)
    dma = pltpu.SemaphoreType.DMA

    def lanes(array):
        return array.reshape(-1, LANES)

    return pl.pallas_call(
        functools.partial(kernel, regions),
        out_shape=(
            jax.ShapeDtypeStruct((nodes, width), BF16),
            jax.ShapeDtypeStruct((fields, points), BF16),
        ),
        in_specs=[vmem, anywhere] + [vmem] * 12 + [anywhere] * 10,
        out_specs=(vmem, vmem),
        scratch_shapes=[pltpu.VMEM((points, width), BF16)]
        + [square] * 9
        + [
            pltpu.VMEM((fields, width), BF16),
            dma((11,)),
            pltpu.VMEM((2, BORDER, width), BF16),
            pltpu.VMEM((2, BORDER, width), BF16),
            pltpu.VMEM((2, BORDER, width), BF16),
            dma((2, 2)),
            dma((2, 2)),
            pltpu.VMEM((regions, COARSE, width), BF16),
            dma((2, line)),
            dma((2, line)),
            dma((line,)),
            dma((line,)),
            dma((2, line)),
            dma((2, line)),
            pltpu.VMEM((span + nodes + TAIL, width), BF16),
            pltpu.VMEM((regions * COARSE, width), BF16),
            pltpu.VMEM((span + TAIL, width), BF16),
            pltpu.VMEM((16, edges), F32),
            pltpu.VMEM((16, slots), F32),
            pltpu.VMEM((3, 16, points), F32),
            pltpu.VMEM((nodes, width), F32),
            pltpu.VMEM((nodes, width), F32),
            pltpu.VMEM((points, width), F32),
            pltpu.VMEM((points, width), F32),
        ],
        compiler_params=pltpu.CompilerParams(
            collective_id=0, has_side_effects=True, vmem_limit_bytes=56 * 1024 * 1024
        ),
        name="graph_round",
    )(
        node_latent,
        grid_latent,
        lanes(fine_edge_sender),
        lanes(short_recv),
        short_geo,
        lanes(long_send),
        lanes(long_recv),
        long_geo,
        dec_send,
        dec_geo,
        w_send,
        w_recv,
        w_edge_geo,
        w_dec_geo,
        w_message,
        w_node_self,
        w_node_agg,
        w_node_out,
        w_dec_send,
        w_dec_grid,
        decoding_link_final_matrix,
        w_grid_agg,
        w_grid_self,
        final_projection_matrix,
    )


def solution(mesh):
    split = ("ens", "region")
    in_specs = (
        P(split, None),
        P(split, None),
        P(split),
        P(split),
        P(None, split),
        P(split),
        P(split),
        P(None, split),
        P(None, split),
        P(None, None, split),
    ) + (P(),) * 14
    out_specs = (P(split, None), P(None, split))
    return jax.shard_map(body, mesh=mesh, in_specs=in_specs, out_specs=out_specs, check_vma=False)
```

time: 134 us -> 38.2 us (0.29)
  matrix products: 41.2 us -> 0 us
  Pallas kernels: 0 us -> 33.4 us
  local copies, waits for them, and re-layouts: 37.1 us -> 3.92 us
  other arithmetic: 25.4 us -> 0 us
  starting transfers between devices: 24.4 us -> 0 us
  waiting for transfers between devices: 3.65 us -> 0 us
    dot_general x19 -> x0, matrix products: 41.2 us -> none  [the longest x13 24 us: product(): return jnp.dot(left, right, preferred_element_type=jnp.float32)]
    pallas_call x0 -> x1, Pallas kernels: none -> 33.4 us  [body(): pl.pallas_call(functools.partial(kernel, regions), out_shape=(jax.ShapeDt...]
    gather x7 -> x0, local copies, waits for them, and re-layouts: 28.4 us -> none  [the longest x1 8.95 us: body(): send_ext[fine_edge_sender - row_offset] + recv_proj[short_recv]]
    scatter-add x2 -> x0, other arithmetic: 17.7 us -> none  [body(): aggregate = jnp.zeros((node_count, channel_count), jnp.float32).at[short_...]
    all_to_all x2 -> x0, starting transfers between devices: 12.5 us -> none  [the longest x1 6.45 us: body(): lax.all_to_all(asked, 'region', split_axis=0, concat_axis=0, tiled=True)]
    ppermute x4 -> x0, starting transfers between devices: 11.9 us -> none  [the longest x2 8.08 us: extended_2(): before = lax.ppermute(last, axis, up)]
    mul x2 -> x0, local copies, waits for them, and re-layouts: 6.9 us -> none  [the longest x1 5.34 us: normalize(): return middle_point * lax.rsqrt(spread + 1e-05)]
    unnamed x34 -> x5, local copies, waits for them, and re-layouts: 0.09 us -> 3.92 us
  transfers between devices with their start and end apart: 6 -> 0, of which waited for: 1 -> 0; matrix products, arithmetic and copies ran while one was open for 50% -> 0% of each run, Pallas kernels for 0% -> 0%
where the time goes in v1:
time: 38.2 us; the launch traced here: 38 us
  Pallas kernels  33.4 us (87%)
  local copies, waits for them, and re-layouts  3.92 us (10%)
  between operations  0.65 us (2%)
    pallas_call x1, Pallas kernels, body(): pl.pallas_call(functools.partial(kernel, regions), out_shape=(jax.ShapeDt...  33.4 us
    unnamed x5, local copies, waits for them, and re-layouts  3.92 us

profile of v1, /device:TPU:1, one launch (start us, length us, event | category | flops | bytes accessed | tf_op | source)
XLA Modules:
  0.0 38.0 jit_solution(17337749918171149367)
XLA Ops:
  0.6 1.4 %copy.26.dec_geo = f32[4,3,512]{2,1,0:T(4,128)} copy(f32[4,3,512]{2,0,1:T(4,128)} %param.33) | data formatting | bytes 49152 | tf_op args[9]
  2.0 33.4 %graph_round.1 = (bf16[512,512]{1,0:T(8,128)(2,1)}, bf16[100,512]{1,0:T(8,128)(2,1)}) custom-call(bf16[512,512]{1,0:T(8,128)(2,1)} %node.1, bf16[512,512]{1,0:T(8,128)(2,1)} %grid_hbm.1, s32[16,128]{1,0:T(8,128)} %bitcast.4, s32[16,128]{1,0:T(8,128)} %bitcast.5, f32[4,2048]{1,0:T(4,128)} %fine_geo.1, s32[4,128]{1,0:T(4,128)} %bitcast.6, s32[4,128]{1,0:T(4,128)} %bitcast.7, ...), custom_call_target="tpu_custom_call" | custom-call | tf_op jit(solution)/shard_map/graph_round/pallas_call | solution.py:477
  35.4 0.0 copy-start
  35.5 1.9 %copy.29 = bf16[512,512]{1,0:T(8,128)(2,1)} copy(bf16[512,512]{1,0:T(8,128)(2,1)} %get-tuple-element.4) | data formatting | bytes 1048576
  37.4 0.0 copy-done
  37.4 0.6 %copy.30 = bf16[100,512]{1,0:T(8,128)(2,1)} copy(bf16[100,512]{1,0:T(8,128)(2,1)S(1)} %copy-done) | data formatting | bytes 204800
Async XLA Ops:
  35.4 1.9 %copy-start = (bf16[100,512]{1,0:T(8,128)(2,1)S(1)}, bf16[100,512]{1,0:T(8,128)(2,1)}, u32[]{:S(2)}) copy-start(bf16[100,512]{1,0:T(8,128)(2,1)} %get-tuple-element.5) | copy-start | bytes 307204

commit v2 on v1

--- a/solution.py
+++ b/solution.py
@@ -131,6 +131,8 @@
     self_part,
     grid_part,
     grid_own,
+    hidden,
+    picks,
 ):
     nodes, width = node.shape
     edges = slab_fine.shape[1]
@@ -263,7 +265,7 @@
                 if step < line - 1:
                     onward = has_next if way == 0 else has_back
                     pl.when(onward)(lambda: z_copy(way, step, place).start())
-                if step > 0 or way == 0:
+                if step > 0:
                     spread(place)
 
     def step_y():
@@ -315,7 +317,7 @@
         slab_dec[k, 0:1, :] = (dec_send[k : k + 1, :] - offset).astype(F32)
         slab_dec[k, 1:4, :] = jnp.zeros((3, points), F32)
         for i in range(4):
-            geo = dec_geo[i, k : k + 1, :]
+            geo = dec_geo[k, i : i + 1, :]
             high = geo.astype(BF16).astype(F32)
             slab_dec[k, 4 + i : 5 + i, :] = high
             slab_dec[k, 8 + i : 9 + i, :] = geo - high
@@ -325,21 +327,38 @@
     self_part[...] = dot(own, w_node_self[...])
     load(1).wait()
 
+    load(0).wait()
+    load(6).wait()
+    grid_part[...] = dot(grid[...], w_dec_grid[...])
+
+    def pick_fine(slab):
+        turned = turn(slab)
+        place = turned[:, 0:2].astype(jnp.int32)
+        return jnp.concatenate(
+            [one_hot(place[:, 0:1], span), one_hot(place[:, 1:2], nodes), turned.astype(BF16)],
+            axis=1,
+        )
+
     settle(node_first, node_last, 0, edge_in)
+    spread(spot)
     border = jnp.concatenate([edge_in[0], edge_in[1]], axis=0)
     border_proj = dot(border, w_send[...]).astype(BF16)
     table[0:BORDER, :] = border_proj[:BORDER]
     table[BORDER + nodes : span, :] = border_proj[BORDER:]
 
-    def add_messages(pre, slab_rows):
-        message = normalize(dot(silu(pre).astype(BF16), w_message[...])).astype(BF16)
-        total[...] += dot(one_hot_rows(slab_rows.astype(jnp.int32), nodes), message)
+    def message_of(held):
+        return normalize(dot(held, w_message[...])).astype(BF16)
+
+    def add(place, message):
+        total[...] += dot(one_hot_rows(place.astype(jnp.int32), nodes), message)
 
     loops = edges // CHUNK
-    steps = [functools.partial(step_z, step) for step in range(1, line)] + [step_y]
+    steps = [functools.partial(step_z, step) for step in range(1, line)]
     turns = [[] for _ in range(loops)]
     for number, step in enumerate(steps):
-        turns[number * loops // len(steps)].append(step)
+        turns[1 + number * (loops - 1) // len(steps)].append(step)
+
+    hidden[...] = silu(dot(pick_fine(slab_fine[:, :CHUNK]), table[...])).astype(BF16)
 
     def fine(i, carry):
         for number, group_of in enumerate(turns):
@@ -351,18 +370,18 @@
                         step()
 
         at = pl.ds(pl.multiple_of(i * CHUNK, CHUNK), CHUNK)
-        slab = slab_fine[:, at]
-        turned = turn(slab)
-        place = turned[:, 0:2].astype(jnp.int32)
-        pick = jnp.concatenate(
-            [one_hot(place[:, 0:1], span), one_hot(place[:, 1:2], nodes), turned.astype(BF16)],
-            axis=1,
-        )
-        add_messages(dot(pick, table[...]), slab[1:2, :])
+        before = pl.ds(pl.multiple_of((i - 1) * CHUNK, CHUNK), CHUNK)
+        held = dot(hidden[...], w_message[...])
+        pre = dot(pick_fine(slab_fine[:, at]), table[...])
+        add(slab_fine[1:2, before], normalize(held).astype(BF16))
+        hidden[...] = silu(pre).astype(BF16)
         return carry
 
-    lax.fori_loop(0, loops, fine, 0)
-
+    lax.fori_loop(1, loops, fine, 0)
+    step_y()
+    add(slab_fine[1:2, edges - CHUNK :], message_of(hidden[...]))
+    load(9).wait()
+    grid_own[...] = dot(grid[...], w_grid_self[...])
     step_end()
     coarse_table[...] = dot(
         coarse[...].reshape(regions * COARSE, width), w_send[...]
@@ -376,7 +395,7 @@
         pre = dot(
             one_hot(place[:, 0:1], reach), coarse_table[number * reach : (number + 1) * reach, :]
         ) + dot(near, table[span:, :])
-        add_messages(pre, slab[1:2, :])
+        add(slab[1:2, :], message_of(silu(pre).astype(BF16)))
 
     load(3).wait()
     load(4).wait()
@@ -396,11 +415,16 @@
     out_mesh[inner, :] = refresh(total[inner, :], self_part[inner, :], node[inner, :])
     out_mesh[:BORDER, :] = ends[:BORDER]
     out_mesh[nodes - BORDER :, :] = ends[BORDER:]
-    for number in (5, 0, 6, 9):
-        load(number).wait()
+    load(5).wait()
     dec_table[BORDER : BORDER + nodes, :] = dot(out_mesh[...], w_dec_send[...]).astype(BF16)
-    grid_part[...] = dot(grid[...], w_dec_grid[...])
-    grid_own[...] = dot(grid[...], w_grid_self[...])
+    part = points // 2
+    for number in range(2):
+        for k in range(3):
+            turned = turn(slab_dec[k, :, number * part : (number + 1) * part])
+            place = turned[:, 0:1].astype(jnp.int32)
+            rows = pl.ds(k * part, part)
+            picks[number, rows, :span] = one_hot(place, span)
+            picks[number, rows, span:] = turned.astype(BF16)
     for number in (7, 8, 10):
         load(number).wait()
     settle(ends_out.at[0], ends_out.at[1], 1, ends_in)
@@ -409,28 +433,34 @@
     dec_table[0:BORDER, :] = border_proj[:BORDER]
     dec_table[BORDER + nodes : span, :] = border_proj[BORDER:]
 
-    part = points // 2
-
     for number in range(2):
         at = pl.ds(number * part, part)
-        picks = []
-        for k in range(3):
-            turned = turn(slab_dec[k, :, at])
-            place = turned[:, 0:1].astype(jnp.int32)
-            picks.append(jnp.concatenate([one_hot(place, span), turned.astype(BF16)], axis=1))
-        pick = jnp.concatenate(picks, axis=0)
         grid_three = jnp.concatenate([grid_part[at, :]] * 3, axis=0)
-        pre = dot(pick, dec_table[...]) + grid_three
+        pre = dot(picks[number], dec_table[...]) + grid_three
         message = normalize(dot(silu(pre).astype(BF16), w_dec_final[...]))
         gathered = message[:part] + message[part : 2 * part] + message[2 * part :]
-        hidden = silu(dot(gathered.astype(BF16), w_grid_agg[...]) + grid_own[at, :])
+        state = silu(dot(gathered.astype(BF16), w_grid_agg[...]) + grid_own[at, :])
         fields = lax.dot_general(
             w_final[...],
-            hidden.astype(BF16),
+            state.astype(BF16),
             (((1,), (1,)), ((), ())),
             preferred_element_type=F32,
         )
         out_fields[:, at] = fields.astype(BF16)
+
+
+def hand_over(mesh_in, fields_in, mesh_out, fields_out, sems):
+    quarter = mesh_in.shape[0] // 4
+    copies = [
+        pltpu.make_async_copy(
+            mesh_in.at[pl.ds(i * quarter, quarter)], mesh_out.at[pl.ds(i * quarter, quarter)], sems.at[i]
+        )
+        for i in range(4)
+    ] + [pltpu.make_async_copy(fields_in, fields_out, sems.at[4])]
+    for copy in copies:
+        copy.start()
+    for copy in copies:
+        copy.wait()
 
 
 def body(
@@ -474,7 +504,7 @@
     def lanes(array):
         return array.reshape(-1, LANES)
 
-    return pl.pallas_call(
+    results = pl.pallas_call(
         functools.partial(kernel, regions),
         out_shape=(
             jax.ShapeDtypeStruct((nodes, width), BF16),
@@ -509,6 +539,8 @@
             pltpu.VMEM((nodes, width), F32),
             pltpu.VMEM((points, width), F32),
             pltpu.VMEM((points, width), F32),
+            pltpu.VMEM((CHUNK, width), BF16),
+            pltpu.VMEM((2, 3 * (points // 2), span + TAIL), BF16),
         ],
         compiler_params=pltpu.CompilerParams(
             collective_id=0, has_side_effects=True, vmem_limit_bytes=56 * 1024 * 1024
@@ -524,7 +556,7 @@
         lanes(long_recv),
         long_geo,
         dec_send,
-        dec_geo,
+        jnp.transpose(dec_geo, (1, 0, 2)),
         w_send,
         w_recv,
         w_edge_geo,
@@ -540,6 +572,15 @@
         w_grid_self,
         final_projection_matrix,
     )
+    return pl.pallas_call(
+        hand_over,
+        out_shape=tuple(jax.ShapeDtypeStruct(array.shape, array.dtype) for array in results),
+        in_specs=[anywhere] * 2,
+        out_specs=(anywhere,) * 2,
+        scratch_shapes=[dma((5,))],
+        compiler_params=pltpu.CompilerParams(vmem_limit_bytes=56 * 1024 * 1024),
+        name="hand_over",
+    )(*results)
 
 
 def solution(mesh):

time: 38.2 us -> 53.8 us (1.41)
  Pallas kernels: 33.4 us -> 53 us
  local copies, waits for them, and re-layouts: 3.92 us -> 0 us
    pallas_call x0 -> x1, Pallas kernels: none -> 20.3 us  [body(): pl.pallas_call(hand_over, out_shape=tuple((jax.ShapeDtypeStruct(array.sha...]
    unnamed x5 -> x0, local copies, waits for them, and re-layouts: 3.92 us -> none
    pallas_call x1, Pallas kernels: 33.4 us -> 32.8 us  [body(): pl.pallas_call(functools.partial(kernel, regions), out_shape=(jax.ShapeDt...]
where the time goes in v2:
time: 53.8 us; the launch traced here: 53.7 us
  Pallas kernels  53 us (99%)
  between operations  0.65 us (1%)
    pallas_call x1, Pallas kernels, body(): pl.pallas_call(functools.partial(kernel, regions), out_shape=(jax.ShapeDt...  32.8 us
    pallas_call x1, Pallas kernels, body(): pl.pallas_call(hand_over, out_shape=tuple((jax.ShapeDtypeStruct(array.sha...  20.3 us

profile of v2, /device:TPU:1, one launch (start us, length us, event | category | flops | bytes accessed | tf_op | source)
XLA Modules:
  0.0 53.7 jit_solution(9274806030710724005)
XLA Ops:
  0.6 32.8 %graph_round.1 = (bf16[512,512]{1,0:T(8,128)(2,1)}, bf16[100,512]{1,0:T(8,128)(2,1)}) custom-call(bf16[512,512]{1,0:T(8,128)(2,1)} %node.1, bf16[512,512]{1,0:T(8,128)(2,1)} %grid_hbm.1, s32[16,128]{1,0:T(8,128)} %bitcast.6, s32[16,128]{1,0:T(8,128)} %bitcast.7, f32[4,2048]{1,0:T(4,128)} %fine_geo.1, s32[4,128]{1,0:T(4,128)} %bitcast.8, s32[4,128]{1,0:T(4,128)} %bitcast.9, ...), custom_call_target="tpu_custom_call" | custom-call | tf_op jit(solution)/shard_map/graph_round/pallas_call | solution.py:507
  33.4 20.3 %hand_over.1 = (bf16[512,512]{1,0:T(8,128)(2,1)}, bf16[100,512]{1,0:T(8,128)(2,1)}) custom-call(bf16[512,512]{1,0:T(8,128)(2,1)} %get-tuple-element.4.mesh_in, bf16[100,512]{1,0:T(8,128)(2,1)} %get-tuple-element.5.fields_in), custom_call_target="tpu_custom_call" | custom-call | tf_op jit(solution)/shard_map/hand_over/pallas_call | solution.py:575

commit v3 on v2

--- a/solution.py
+++ b/solution.py
@@ -44,12 +44,22 @@
 
 
 def turn(slab):
-    parts = []
-    for start in range(0, slab.shape[1], LANES):
-        piece = slab[:, start : start + LANES]
-        full = jnp.concatenate([piece, jnp.zeros((LANES - 16, LANES), F32)], axis=0)
-        parts.append(full.T)
-    return jnp.concatenate(parts, axis=0)
+    blocks = slab.shape[1] // LANES
+    pieces = [slab[:, i * LANES : (i + 1) * LANES] for i in range(blocks)]
+    if blocks < LANES // 16:
+        pieces.append(jnp.zeros((LANES - 16 * blocks, LANES), F32))
+    turned = jnp.concatenate(pieces, axis=0).T
+    lanes = lax.broadcasted_iota(jnp.int32, (LANES, LANES), 1)
+    parts = [
+        jnp.where((lanes >= 16 * i) & (lanes < 16 * i + 16), turned, 0.0) for i in range(blocks)
+    ]
+    places = [
+        jnp.concatenate(
+            [turned[:, 16 * i + j : 16 * i + j + 1] for i in range(blocks)], axis=0
+        ).astype(jnp.int32)
+        for j in range(2)
+    ]
+    return jnp.concatenate(parts, axis=0).astype(BF16), places[0], places[1]
 
 
 def put_geometry(slab, geo):
@@ -63,8 +73,7 @@
     high = w_geo.astype(BF16).astype(F32)
     width = w_geo.shape[1]
     rows = jnp.concatenate(
-        [jnp.zeros((4, width), F32), high, high, w_geo - high, jnp.zeros((TAIL - 16, width), F32)],
-        axis=0,
+        [jnp.zeros((4, width), F32), high, high, w_geo - high] * (TAIL // 16), axis=0
     )
     table[start : start + TAIL, :] = rows.astype(BF16)
 
@@ -332,12 +341,8 @@
     grid_part[...] = dot(grid[...], w_dec_grid[...])
 
     def pick_fine(slab):
-        turned = turn(slab)
-        place = turned[:, 0:2].astype(jnp.int32)
-        return jnp.concatenate(
-            [one_hot(place[:, 0:1], span), one_hot(place[:, 1:2], nodes), turned.astype(BF16)],
-            axis=1,
-        )
+        tail, sender, receiver = turn(slab)
+        return jnp.concatenate([one_hot(sender, span), one_hot(receiver, nodes), tail], axis=1)
 
     settle(node_first, node_last, 0, edge_in)
     spread(spot)
@@ -389,11 +394,10 @@
     reach = owners * COARSE
     for number in range(slots // group):
         slab = slab_long[:, number * group : (number + 1) * group]
-        turned = turn(slab)
-        place = turned[:, 0:2].astype(jnp.int32)
-        near = jnp.concatenate([one_hot(place[:, 1:2], nodes), turned.astype(BF16)], axis=1)
+        tail, sender, receiver = turn(slab)
+        near = jnp.concatenate([one_hot(receiver, nodes), tail], axis=1)
         pre = dot(
-            one_hot(place[:, 0:1], reach), coarse_table[number * reach : (number + 1) * reach, :]
+            one_hot(sender, reach), coarse_table[number * reach : (number + 1) * reach, :]
         ) + dot(near, table[span:, :])
         add(slab[1:2, :], message_of(silu(pre).astype(BF16)))
 
@@ -419,12 +423,10 @@
     dec_table[BORDER : BORDER + nodes, :] = dot(out_mesh[...], w_dec_send[...]).astype(BF16)
     part = points // 2
     for number in range(2):
-        for k in range(3):
-            turned = turn(slab_dec[k, :, number * part : (number + 1) * part])
-            place = turned[:, 0:1].astype(jnp.int32)
-            rows = pl.ds(k * part, part)
-            picks[number, rows, :span] = one_hot(place, span)
-            picks[number, rows, span:] = turned.astype(BF16)
+        span_of = slice(number * part, (number + 1) * part)
+        tail, sender, _ = turn(jnp.concatenate([slab_dec[k, :, span_of] for k in range(3)], axis=1))
+        picks[number, :, :span] = one_hot(sender, span)
+        picks[number, :, span:] = tail
     for number in (7, 8, 10):
         load(number).wait()
     settle(ends_out.at[0], ends_out.at[1], 1, ends_in)
@@ -450,13 +452,10 @@
 
 
 def hand_over(mesh_in, fields_in, mesh_out, fields_out, sems):
-    quarter = mesh_in.shape[0] // 4
-    copies = [
-        pltpu.make_async_copy(
-            mesh_in.at[pl.ds(i * quarter, quarter)], mesh_out.at[pl.ds(i * quarter, quarter)], sems.at[i]
-        )
-        for i in range(4)
-    ] + [pltpu.make_async_copy(fields_in, fields_out, sems.at[4])]
+    copies = (
+        pltpu.make_async_copy(mesh_in, mesh_out, sems.at[0]),
+        pltpu.make_async_copy(fields_in, fields_out, sems.at[1]),
+    )
     for copy in copies:
         copy.start()
     for copy in copies:
@@ -576,8 +575,8 @@
         hand_over,
         out_shape=tuple(jax.ShapeDtypeStruct(array.shape, array.dtype) for array in results),
         in_specs=[anywhere] * 2,
-        out_specs=(anywhere,) * 2,
-        scratch_shapes=[dma((5,))],
+        out_specs=(vmem,) * 2,
+        scratch_shapes=[dma((2,))],
         compiler_params=pltpu.CompilerParams(vmem_limit_bytes=56 * 1024 * 1024),
         name="hand_over",
     )(*results)

time: 53.8 us -> 35.4 us (0.66)
  Pallas kernels: 53 us -> 34.6 us
    pallas_call x1, Pallas kernels: 20.3 us -> 1.89 us  [body(): pl.pallas_call(hand_over, out_shape=tuple((jax.ShapeDtypeStruct(array.sha...]
where the time goes in v3:
time: 35.4 us; the launch traced here: 35.3 us
  Pallas kernels  34.6 us (98%)
  between operations  0.65 us (2%)
    pallas_call x1, Pallas kernels, body(): pl.pallas_call(functools.partial(kernel, regions), out_shape=(jax.ShapeDt...  32.7 us
    pallas_call x1, Pallas kernels, body(): pl.pallas_call(hand_over, out_shape=tuple((jax.ShapeDtypeStruct(array.sha...  1.89 us

profile of v3, /device:TPU:1, one launch (start us, length us, event | category | flops | bytes accessed | tf_op | source)
XLA Modules:
  0.0 35.3 jit_solution(4915107934961405805)
XLA Ops:
  0.6 32.7 %graph_round.1 = (bf16[512,512]{1,0:T(8,128)(2,1)}, bf16[100,512]{1,0:T(8,128)(2,1)}) custom-call(bf16[512,512]{1,0:T(8,128)(2,1)} %node.1, bf16[512,512]{1,0:T(8,128)(2,1)} %grid_hbm.1, s32[16,128]{1,0:T(8,128)} %bitcast.6, s32[16,128]{1,0:T(8,128)} %bitcast.7, f32[4,2048]{1,0:T(4,128)} %fine_geo.1, s32[4,128]{1,0:T(4,128)} %bitcast.8, s32[4,128]{1,0:T(4,128)} %bitcast.9, ...), custom_call_target="tpu_custom_call" | custom-call | tf_op jit(solution)/shard_map/graph_round/pallas_call | solution.py:506
  33.4 1.9 %hand_over.1 = (bf16[512,512]{1,0:T(8,128)(2,1)}, bf16[100,512]{1,0:T(8,128)(2,1)}) custom-call(bf16[512,512]{1,0:T(8,128)(2,1)} %get-tuple-element.4.mesh_in, bf16[100,512]{1,0:T(8,128)(2,1)} %get-tuple-element.5.fields_in), custom_call_target="tpu_custom_call" | custom-call | tf_op jit(solution)/shard_map/hand_over/pallas_call | solution.py:574
